TPU v7x, 32 devices: a whole 2x2x4 slice. The times are simulated.
32 devices in a mesh: inl: 8 (over z, y), off: 4 (over x, core).
Axes of the slice: x: 2, y: 2, z: 4, core: 2. Of those that a mesh axis runs over, the one named last changes fastest.
Arguments:
- traces: bfloat16 [4, 4096, 4096], P('off', 'inl'), may hold values from -24 to 24, as said below
- owner: int32 [4, 4096, 1], P('off', 'inl'), may hold values from 0 to 7; in each aligned block of 512 rows (0 to 511, 512 to 1023, ..., all dimensions but the last counted through in order) at most 192 rows name the same one
- local_bin: int32 [4, 4096], P('off', 'inl'), may hold values from 0 to 63
- live_count: int32 [4, 8], P('off', 'inl'), may hold values from 256 to 512, as said below
- xl_gain: float32 [16], replicated, may hold values from 0.2 to 1
- il_gain: float32 [32], replicated, may hold values from 0.2 to 1
Outputs:
- volume: bfloat16 [4, 16, 32, 4096], P('off', 'inl')
Inputs may be any that keep to these rules, and one draw needn't show every extreme that they name: `traces`: every trace amplitude lies in this range. Among the traces of one device no owner is named more than 192 times; some device names one owner exactly 192 times. The first live_count traces of a device are live; some device has all 512 traces live.
All inputs are finite; a program needn't handle non-finite values.
Results may differ from a plain program's by a relative error of at most 0.024.
Values may be sent and summed in bfloat16 or wider, within the bound.
A program may use at most 128 MiB of HBM per device.

v0:
```python
import math
import jax
import jax.numpy as jnp
from jax import lax
from jax.sharding import PartitionSpec as P

NLAG = 80
damping = 0.1


def levinson(series):
    order = series.shape[0]
    error = series[0] + damping
    coeffs = jnp.zeros_like(series).at[0].set(1.0)
    for section in range(1, order):
        partial_sum = jnp.sum(coeffs[:section] * series[section:0:-1], axis=0)
        reflection = -partial_sum / error
        update = coeffs[: section + 1] + reflection * coeffs[section::-1]
        coeffs = coeffs.at[: section + 1].set(update)
        error = error * (1.0 - reflection * reflection)
    return coeffs


def smooth_matrix(gain, reach):
    width = gain.shape[0]
    index = jnp.arange(width)
    distance = jnp.abs(index[:, None] - index[None, :])
    weight = jnp.take(gain, distance) * jnp.exp(-distance.astype(gain.dtype) / reach)
    return (weight / jnp.sum(weight, axis=1, keepdims=True)).astype(jnp.bfloat16)


def autocorrelate(block_rows):
    number, samples = block_rows.shape
    groups = samples // 128

    def autocorrelate_one_block(part_rows):
        height = part_rows.shape[0]
        leading = part_rows.reshape(height, groups, 128)
        following = jnp.pad(part_rows[:, 128:], ((0, 0), (0, 128))).reshape(height, groups, 128)
        within = jnp.einsum("nab,nac->nbc", leading, leading, preferred_element_type=jnp.float32)
        across = jnp.einsum("nab,nac->nbc", leading, following, preferred_element_type=jnp.float32)
        total = within[:, 0, :]
        for offset in range(1, 128):
            total = total + jnp.concatenate(
                [within[:, offset, offset:], across[:, offset, :offset]], axis=1
            )
        return total

    block = math.gcd(number, 64)
    result = lax.map(autocorrelate_one_block, block_rows.reshape(number // block, block, samples))
    return result.reshape(number, 128)


def apply_filter(stacked, filters):
    number, samples = stacked.shape
    taps = filters.shape[1]
    groups = samples // 128
    column = jnp.arange(256)[None, :, None]
    output_pos = jnp.arange(128)[None, None, :]
    lag_index = jnp.arange(taps)[:, None, None]
    table = (column == output_pos + 128 - lag_index).astype(jnp.bfloat16)

    def apply_one_block(pair):
        part_rows, part_filters = pair
        height = part_rows.shape[0]
        kernel = jnp.einsum(
            "nj,jcb->ncb", part_filters, table, preferred_element_type=jnp.float32
        ).astype(jnp.bfloat16)
        padded = jnp.pad(part_rows, ((0, 0), (128, 0))).reshape(height, groups + 1, 128)
        windows = jnp.concatenate([padded[:, :-1], padded[:, 1:]], axis=2)
        result = jnp.einsum("nac,ncb->nab", windows, kernel, preferred_element_type=jnp.float32)
        return result.reshape(height, samples).astype(jnp.bfloat16)

    block = math.gcd(number, 64)
    result = lax.map(
        apply_one_block,
        (
            stacked.reshape(number // block, block, samples),
            filters.reshape(number // block, block, taps),
        ),
    )
    return result.reshape(number, samples)


def shards(traces, owner, local_bin, live_count, xl_gain, il_gain):
    devices = lax.axis_size("inl")
    traces_here = traces.shape[1]
    samples = traces.shape[2]
    shot_rows = traces[0]
    slots = max(2, 3 * traces_here // devices)
    crosslines = xl_gain.shape[0]
    inlines = il_gain.shape[0]
    inline_dev = inlines // devices
    bins_here = inline_dev * crosslines
    destination = owner[0, :, 0]
    alive = jnp.arange(traces_here, dtype=jnp.int32) < live_count[0, 0]
    target = jnp.where(alive, local_bin[0], -1)
    matches = (destination[:, None] == jnp.arange(devices, dtype=jnp.int32)[None, :]).astype(
        jnp.int32
    )
    places = jnp.sum((jnp.cumsum(matches, axis=0) - matches) * matches, axis=1)
    position = destination * slots + places
    source_slot = (
        jnp.full((devices * slots,), traces_here, jnp.int32)
        .at[position]
        .set(jnp.arange(traces_here, dtype=jnp.int32))
    )
    send_bins = jnp.take(target, source_slot, axis=0, mode="fill", fill_value=-1)
    send_rows = jnp.take(shot_rows, source_slot, axis=0, mode="fill", fill_value=0)
    arrived, arrived_bins = (
        lax.all_to_all(
            send_rows.reshape(devices, slots, samples),
            "inl",
            split_axis=0,
            concat_axis=0,
            tiled=True,
        ),
        lax.all_to_all(
            send_bins.reshape(devices, slots), "inl", split_axis=0, concat_axis=0, tiled=True
        ),
    )
    arrived = arrived.reshape(devices * slots, samples)
    arrived_lags = autocorrelate(arrived)
    arrived_bins = arrived_bins.reshape(devices * slots)
    onehot = arrived_bins[:, None] == jnp.arange(bins_here, dtype=jnp.int32)[None, :]
    counts = jnp.sum(onehot.astype(jnp.float32), axis=0)
    contract = (((0,), (0,)), ((), ()))
    stack_sum = lax.dot_general(
        onehot.astype(jnp.bfloat16), arrived, contract, preferred_element_type=jnp.float32
    )
    lag_sum = lax.dot_general(
        onehot.astype(jnp.float32),
        arrived_lags[:, :NLAG],
        contract,
        precision=lax.Precision.HIGHEST,
        preferred_element_type=jnp.float32,
    )
    lag_total = lax.psum(lag_sum.astype(jnp.bfloat16), "off").astype(jnp.float32)
    stacked = (stack_sum / jnp.maximum(counts, 1.0)[:, None]).astype(jnp.bfloat16)
    rho = lag_total / jnp.maximum(lag_total[:, :1], 1.0)
    filters = levinson(rho.T).T.astype(jnp.bfloat16)
    decon = apply_filter(stacked, filters)
    cross_matrix = smooth_matrix(xl_gain, crosslines / 16.0)
    smoothed = jnp.einsum(
        "xy,iyt->ixt",
        cross_matrix,
        decon.reshape(inline_dev, crosslines, samples),
        preferred_element_type=jnp.float32,
    ).astype(jnp.bfloat16)
    relaid = lax.all_to_all(smoothed, "inl", split_axis=1, concat_axis=0, tiled=True)
    inline_matrix = smooth_matrix(il_gain, 2.0 * inline_dev)
    result = jnp.einsum(
        "ij,jxt->xit", inline_matrix, relaid, preferred_element_type=jnp.float32
    ).astype(jnp.bfloat16)
    return result[None]


def solution(mesh):
    placed = (
        P("off", "inl", None),
        P("off", "inl", None),
        P("off", "inl"),
        P("off", "inl"),
        P(),
        P(),
    )
    return jax.shard_map(
        shards, mesh=mesh, in_specs=placed, out_specs=P("off", "inl", None, None), check_vma=False
    )
```

profile of v0, /device:TPU:0, one launch (start us, length us, event | category | flops | bytes accessed | tf_op | source)
XLA Modules:
  0.0 1120.3 jit_solution(14159218616566697119)
XLA Ops:
  3.6 2.4 scatter_custom_fusion
  7.4 9.5 gather_fusion
  17.5 7.3 all-to-all-start
  24.9 24.8 %gather_fusion.1 = bf16[1536,4096]{1,0:T(8,128)(2,1)} fusion(bf16[512,4096]{1,0:T(8,128)(2,1)} %bitcast.1481, s32[2048]{0:T(1024)S(1)} %pad_clamp_fusion), kind=kCustom, calls=%fused_computation.1 | custom fusion | bytes 25171968 | tf_op jit(solution)/shard_map/jit(_take)/gather | solution.py:109
  49.7 10.7 broadcast_select_fusion
  60.3 6.1 all-to-all-start.1
  68.9 270.0 %all-to-all-done.1 = bf16[8,192,4096]{2,1,0:T(8,128)(2,1)} async-done(((bf16[8,192,4096]{2,1,0:T(8,128)(2,1)}), bf16[8,192,4096]{2,1,0:T(8,128)(2,1)}, u32[]{:S(2)}, u32[]{:S(2)}) %all-to-all-start.1) | async-done | bytes 12582944 | tf_op jit(solution)/shard_map/all_to_all | solution.py:111
  339.0 706.3 %while.97 = (s32[]{:T(128)}, f32[24,64,128]{2,1,0:T(8,128)S(1)}, bf16[24,64,4096]{2,1,0:T(8,128)(2,1)}, s32[]{:T(128)}) while((s32[]{:T(128)}, f32[24,64,128]{2,1,0:T(8,128)S(1)}, bf16[24,64,4096]{2,1,0:T(8,128)(2,1)}, s32[]{:T(128)}) %tuple.473), condition=%wide.region_6.7_spmd, body=%wide.region_5.6_spmd.sunk | while | flops 136298496 | bytes 32456764 | solution.py:50
  453.0 2.3 fusion.197
  511.1 2.3 fusion.197
  540.1 2.3 fusion.197
  569.1 2.3 fusion.197
  598.2 2.3 fusion.197
  627.2 2.3 fusion.197
  656.3 2.3 fusion.197
  685.3 2.3 fusion.197
  714.4 2.3 fusion.197
  743.4 2.3 fusion.197
  772.5 2.3 fusion.197
  801.5 2.3 fusion.197
  830.5 2.3 fusion.197
  859.6 2.3 fusion.197
  888.6 2.3 fusion.197
  946.7 2.3 fusion.197
  1004.8 2.3 fusion.197
  1046.0 10.3 psum.7
  1083.9 6.9 fusion.124
  1091.5 2.7 fusion.129
  1094.1 4.1 fusion.130
  1100.0 4.7 all-to-all-start.2
  1104.8 6.6 gather_fusion.3
  1111.5 7.0 all-to-all-done.2
  (6879 shorter events, 645.4 us)
Async XLA Ops:
  0.0 1104.8 %copy-start = (f32[32]{0:T(128)S(1)}, f32[32]{0:T(128)}, u32[]{:S(2)}) copy-start(f32[32]{0:T(128)} %param.175) | copy-start | bytes 388
  17.5 42.8 %all-to-all-start = ((s32[8,1,192]{2,1,0:T(1,128)}), s32[8,1,192]{2,1,0:T(1,128)S(1)}, u32[]{:S(2)}, u32[]{:S(2)}) async-start(s32[8,1,192]{2,1,0:T(1,128)} %select_n.89), calls=%async_computation | async-start | bytes 16384 | tf_op jit(solution)/shard_map/all_to_all | solution.py:118
  60.3 6.2 copy-start.1
  60.3 278.6 %all-to-all-start.1 = ((bf16[8,192,4096]{2,1,0:T(8,128)(2,1)}), bf16[8,192,4096]{2,1,0:T(8,128)(2,1)}, u32[]{:S(2)}, u32[]{:S(2)}) async-start(bf16[8,192,4096]{2,1,0:T(8,128)(2,1)} %broadcast_select_fusion), calls=%async_computation.1 | async-start | bytes 25165824 | tf_op jit(solution)/shard_map/all_to_all | solution.py:111
  338.9 718.5 %copy-start.2 = (f32[80,64]{1,0:T(8,128)S(1)}, f32[80,64]{1,0:T(8,128)}, u32[]{:S(2)}) copy-start(f32[80,64]{1,0:T(8,128)} %constant.1976.clone.1) | copy-start | bytes 61444
  338.9 718.5 %copy-start.3 = (f32[2,64]{1,0:T(2,128)S(1)}, f32[2,64]{1,0:T(2,128)}, u32[]{:S(2)}) copy-start(f32[2,64]{1,0:T(2,128)} %constant.1978.clone.1) | copy-start | bytes 1540
  338.9 718.5 %copy-start.4 = (f32[2,64]{1,0:T(2,128)S(1)}, f32[2,64]{1,0:T(2,128)}, u32[]{:S(2)}) copy-start(f32[2,64]{1,0:T(2,128)} %constant.1979.clone.1) | copy-start | bytes 1540
  1100.0 18.5 %all-to-all-start.2 = ((bf16[4,16,4096]{2,0,1:T(4,128)(2,1)}), bf16[4,16,4096]{2,0,1:T(4,128)(2,1)S(1)}, u32[]{:S(2)}, u32[]{:S(2)}) async-start(bf16[4,16,4096]{2,0,1:T(4,128)(2,1)} %copy.1305), calls=%async_computation.2 | async-start | bytes 1048576 | tf_op jit(solution)/shard_map/all_to_all | solution.py:150
where the time goes:
time: 1130 us; the launch traced here: 1120 us
  local copies, waits for them, and re-layouts  626 us (55%)
  waiting for transfers between devices  277 us (25%)
  other arithmetic  73.6 us (7%)
  loops' own time  59.2 us (5%)
  matrix products  52.5 us (5%)
  starting transfers between devices  18.1 us (2%)
    slice x3048, local copies, waits for them, and re-layouts, autocorrelate_one_block(): within[:, offset, offset:]  406 us
    all_to_all x1, waiting for transfers between devices, shards(): lax.all_to_all(send_rows.reshape(devices, slots, samples), 'inl', split_a...  270 us
    slice x3048, local copies, waits for them, and re-layouts, autocorrelate_one_block(): across[:, offset, :offset]  113 us
    another operation x1, loops' own time, autocorrelate(): lax.map(autocorrelate_one_block, block_rows.reshape(number // block, bloc...  59.2 us
    dynamic_update_slice x24, other arithmetic, autocorrelate(): lax.map(autocorrelate_one_block, block_rows.reshape(number // block, bloc...  55.5 us
    squeeze x24, local copies, waits for them, and re-layouts, autocorrelate(): lax.map(autocorrelate_one_block, block_rows.reshape(number // block, bloc...  28.3 us
    gather x1, local copies, waits for them, and re-layouts, shards(): jnp.take(shot_rows, source_slot, axis=0, mode='fill', fill_value=0)  24.8 us

commit v1 on v0

--- a/solution.py
+++ b/solution.py
@@ -6,6 +6,29 @@
 
 NLAG = 80
 damping = 0.1
+
+
+def cut_along(x, dim, size):
+    shape = x.shape
+    pieces = x.reshape(*shape[:dim], size, shape[dim] // size, *shape[dim + 1 :])
+    return jnp.moveaxis(pieces, dim, 0)
+
+
+def in_order(blocks, dim):
+    dims = list(blocks.shape[1:])
+    dims[dim] *= blocks.shape[0]
+    return jnp.moveaxis(blocks, 0, dim).reshape(dims)
+
+
+def pairwise_exchange(array, axis, split_dim, concat_dim):
+    length, here = (lax.axis_size(axis), lax.axis_index(axis))
+    pieces = cut_along(array, split_dim, length)
+    outs = [pieces[here]]
+    for step in range(1, length):
+        sent = pieces[here ^ step]
+        outs.append(lax.ppermute(sent, axis, [(i, i ^ step) for i in range(length)]))
+    pieces = jnp.stack(outs)[here ^ jnp.arange(length)]
+    return in_order(pieces, concat_dim)
 
 
 def levinson(series):
@@ -108,13 +131,7 @@
     send_bins = jnp.take(target, source_slot, axis=0, mode="fill", fill_value=-1)
     send_rows = jnp.take(shot_rows, source_slot, axis=0, mode="fill", fill_value=0)
     arrived, arrived_bins = (
-        lax.all_to_all(
-            send_rows.reshape(devices, slots, samples),
-            "inl",
-            split_axis=0,
-            concat_axis=0,
-            tiled=True,
-        ),
+        pairwise_exchange(send_rows.reshape(devices, slots, samples), "inl", 0, 0),
         lax.all_to_all(
             send_bins.reshape(devices, slots), "inl", split_axis=0, concat_axis=0, tiled=True
         ),

time: 1130 us -> 1140 us (level)
  waiting for transfers between devices: 277 us -> 189 us
  starting transfers between devices: 18.1 us -> 87.6 us
  local copies, waits for them, and re-layouts: 626 us -> 655 us
    all_to_all x1 -> x0, waiting for transfers between devices: 270 us -> none  [shards(): lax.all_to_all(send_rows.reshape(devices, slots, samples), 'inl', split_a...]
    all_to_all x1, waiting for transfers between devices: 0.01 us -> 127 us  [shards(): lax.all_to_all(send_bins.reshape(devices, slots), 'inl', split_axis=0, co...]
    all_to_all x1, starting transfers between devices: 4.67 us -> 70 us  [shards(): lax.all_to_all(smoothed, 'inl', split_axis=1, concat_axis=0, tiled=True)]
    ppermute x0 -> x7, waiting for transfers between devices: none -> 54.5 us  [pairwise_exchange(): lax.ppermute(sent, axis, [(i, i ^ step) for i in range(length)])]
    ppermute x0 -> x7, starting transfers between devices: none -> 12.7 us  [pairwise_exchange(): lax.ppermute(sent, axis, [(i, i ^ step) for i in range(length)])]
    unnamed x10 -> x18, local copies, waits for them, and re-layouts: 0.02 us -> 12 us
where the time goes in v1:
time: 1140 us; the launch traced here: 1130 us
  local copies, waits for them, and re-layouts  655 us (57%)
  waiting for transfers between devices  189 us (17%)
  starting transfers between devices  87.6 us (8%)
  other arithmetic  69.3 us (6%)
  loops' own time  59.2 us (5%)
  matrix products  52.5 us (5%)
    slice x3048, local copies, waits for them, and re-layouts, autocorrelate_one_block(): within[:, offset, offset:]  406 us
    all_to_all x1, waiting for transfers between devices, shards(): lax.all_to_all(send_bins.reshape(devices, slots), 'inl', split_axis=0, co...  127 us
    slice x3048, local copies, waits for them, and re-layouts, autocorrelate_one_block(): across[:, offset, :offset]  113 us
    all_to_all x1, starting transfers between devices, shards(): lax.all_to_all(smoothed, 'inl', split_axis=1, concat_axis=0, tiled=True)  70 us
    another operation x1, loops' own time, autocorrelate(): lax.map(autocorrelate_one_block, block_rows.reshape(number // block, bloc...  59.2 us
    dynamic_update_slice x24, other arithmetic, autocorrelate(): lax.map(autocorrelate_one_block, block_rows.reshape(number // block, bloc...  55.5 us
    ppermute x7, waiting for transfers between devices, pairwise_exchange(): lax.ppermute(sent, axis, [(i, i ^ step) for i in range(length)])  54.5 us
    squeeze x24, local copies, waits for them, and re-layouts, autocorrelate(): lax.map(autocorrelate_one_block, block_rows.reshape(number // block, bloc...  28.3 us

profile of v1, /device:TPU:0, one launch (start us, length us, event | category | flops | bytes accessed | tf_op | source)
XLA Modules:
  0.0 1126.8 jit_solution(605811684133529745)
XLA Ops:
  3.6 2.4 scatter_custom_fusion
  7.4 9.5 gather_fusion
  16.9 24.8 %gather_fusion.1 = bf16[1536,4096]{1,0:T(8,128)(2,1)} fusion(bf16[512,4096]{1,0:T(8,128)(2,1)} %bitcast.1512, s32[2048]{0:T(1024)S(1)} %pad_clamp_fusion), kind=kCustom, calls=%fused_computation.1 | custom fusion | bytes 25171968 | tf_op jit(solution)/shard_map/jit(_take)/gather | solution.py:132
  41.7 6.3 broadcast_select_fusion
  48.1 4.6 dynamic-slice_bitcast_fusion.2
  52.7 3.0 collective-permute-start
  57.3 3.0 collective-permute-start.3
  62.2 4.9 all-to-all-start
  69.4 126.9 %all-to-all-done = s32[8,1,192]{2,1,0:T(1,128)S(1)} async-done(((s32[8,1,192]{2,1,0:T(1,128)}), s32[8,1,192]{2,1,0:T(1,128)S(1)}, u32[]{:S(2)}, u32[]{:S(2)}) %all-to-all-start) | async-done | bytes 6176 | tf_op jit(solution)/shard_map/all_to_all | solution.py:135
  196.6 3.7 collective-permute-start.5
  200.3 2.7 bitcast_dynamic-update-slice_fusion.6
  203.2 2.7 bitcast_dynamic-update-slice_fusion.5
  205.9 2.7 bitcast_dynamic-update-slice_fusion.4
  211.2 24.8 %collective-permute-done.5 = bf16[1,192,4096]{2,1,0:T(8,128)(2,1)S(1)} collective-permute-done((bf16[1,192,4096]{2,1,0:T(8,128)(2,1)}, bf16[1,192,4096]{2,1,0:T(8,128)(2,1)S(1)}, u32[]{:S(2)}, u32[]{:S(2)}) %collective-permute-start.5) | collective-permute-done | bytes 1572896 | tf_op jit(solution)/shard_map/ppermute | solution.py:29
  237.4 29.6 %collective-permute-done.6 = bf16[1,192,4096]{2,1,0:T(8,128)(2,1)S(1)} collective-permute-done((bf16[1,192,4096]{2,1,0:T(8,128)(2,1)}, bf16[1,192,4096]{2,1,0:T(8,128)(2,1)S(1)}, u32[]{:S(2)}, u32[]{:S(2)}) %collective-permute-start.6) | collective-permute-done | bytes 1572896 | tf_op jit(solution)/shard_map/ppermute | solution.py:29
  268.2 11.0 gather_fusion.2
  279.2 706.3 %while.97 = (s32[]{:T(128)}, f32[24,64,128]{2,1,0:T(8,128)S(1)}, bf16[24,64,4096]{2,1,0:T(8,128)(2,1)}, s32[]{:T(128)}) while((s32[]{:T(128)}, f32[24,64,128]{2,1,0:T(8,128)S(1)}, bf16[24,64,4096]{2,1,0:T(8,128)(2,1)}, s32[]{:T(128)}) %tuple.485), condition=%wide.region_6.7_spmd, body=%wide.region_5.6_spmd.sunk | while | flops 136298496 | bytes 32456764 | solution.py:73
  335.2 2.3 fusion.197
  364.2 2.3 fusion.197
  393.3 2.3 fusion.197
  422.3 2.3 fusion.197
  451.3 2.3 fusion.197
  480.4 2.3 fusion.197
  509.4 2.3 fusion.197
  567.5 2.3 fusion.197
  986.3 10.3 psum.7
  1024.2 6.9 fusion.124
  1031.7 2.7 fusion.129
  1034.4 4.1 fusion.130
  1040.3 70.0 %all-to-all-start.1 = ((bf16[4,16,4096]{2,0,1:T(4,128)(2,1)}), bf16[4,16,4096]{2,0,1:T(4,128)(2,1)S(1)}, u32[]{:S(2)}, u32[]{:S(2)}) async-start(bf16[4,16,4096]{2,0,1:T(4,128)(2,1)} %copy.1305), calls=%async_computation.1 | async-start | bytes 1048576 | tf_op jit(solution)/shard_map/all_to_all | solution.py:167
  1110.3 6.6 gather_fusion.4
  1117.1 8.0 all-to-all-done.1
  (6903 shorter events, 674.5 us)
Async XLA Ops:
  0.0 1110.3 %copy-start = (f32[32]{0:T(128)S(1)}, f32[32]{0:T(128)}, u32[]{:S(2)}) copy-start(f32[32]{0:T(128)} %param.175) | copy-start | bytes 388
  48.0 19.3 %copy-start.1 = (f32[16]{0:T(128)S(1)}, f32[16]{0:T(128)}, u32[]{:S(2)}) copy-start(f32[16]{0:T(128)} %param.174) | copy-start | bytes 196
  52.7 143.9 %collective-permute-start = (bf16[1,192,4096]{2,1,0:T(8,128)(2,1)}, bf16[1,192,4096]{2,1,0:T(8,128)(2,1)}, u32[]{:S(2)}, u32[]{:S(2)}) collective-permute-start(bf16[1,192,4096]{2,1,0:T(8,128)(2,1)} %get-tuple-element.1258), channel_id=1, source_target_pairs={{0,4},{4,0},{8,12},{12,8},{16,20},{20,16},{24,28},{28,24},{1,5},{5... | collective-permute-start | bytes 4718600 | tf_op jit(solution)/shard_map/ppermute | solution.py:29
  55.7 147.3 %collective-permute-start.1 = (bf16[1,192,4096]{2,1,0:T(8,128)(2,1)}, bf16[1,192,4096]{2,1,0:T(8,128)(2,1)}, u32[]{:S(2)}, u32[]{:S(2)}) collective-permute-start(bf16[1,192,4096]{2,1,0:T(8,128)(2,1)} %get-tuple-element.1257), channel_id=1, source_target_pairs={{0,8},{4,12},{8,0},{12,4},{16,24},{20,28},{24,16},{28,20},{1,9},{5... | collective-permute-start | bytes 4718600 | tf_op jit(solution)/shard_map/ppermute | solution.py:29
  57.3 148.6 %collective-permute-start.2 = (bf16[1,192,4096]{2,1,0:T(8,128)(2,1)}, bf16[1,192,4096]{2,1,0:T(8,128)(2,1)}, u32[]{:S(2)}, u32[]{:S(2)}) collective-permute-start(bf16[1,192,4096]{2,1,0:T(8,128)(2,1)} %get-tuple-element.1256), channel_id=1, source_target_pairs={{0,12},{4,8},{8,4},{12,0},{16,28},{20,24},{24,20},{28,16},{1,13},{... | collective-permute-start | bytes 4718600 | tf_op jit(solution)/shard_map/ppermute | solution.py:29
  57.3 151.4 %collective-permute-start.3 = (bf16[1,192,4096]{2,1,0:T(8,128)(2,1)}, bf16[1,192,4096]{2,1,0:T(8,128)(2,1)S(1)}, u32[]{:S(2)}, u32[]{:S(2)}) collective-permute-start(bf16[1,192,4096]{2,1,0:T(8,128)(2,1)} %get-tuple-element.1255), channel_id=1, source_target_pairs={{0,16},{4,20},{8,24},{12,28},{16,0},{20,4},{24,8},{28,12},{1,17},{... | collective-permute-start | bytes 4718600 | tf_op jit(solution)/shard_map/ppermute | solution.py:29
  60.2 149.7 %collective-permute-start.4 = (bf16[1,192,4096]{2,1,0:T(8,128)(2,1)}, bf16[1,192,4096]{2,1,0:T(8,128)(2,1)S(1)}, u32[]{:S(2)}, u32[]{:S(2)}) collective-permute-start(bf16[1,192,4096]{2,1,0:T(8,128)(2,1)} %get-tuple-element.1254), channel_id=1, source_target_pairs={{0,20},{4,16},{8,28},{12,24},{16,4},{20,0},{24,12},{28,8},{1,21},{... | collective-permute-start | bytes 4718600 | tf_op jit(solution)/shard_map/ppermute | solution.py:29
  62.2 134.1 %all-to-all-start = ((s32[8,1,192]{2,1,0:T(1,128)}), s32[8,1,192]{2,1,0:T(1,128)S(1)}, u32[]{:S(2)}, u32[]{:S(2)}) async-start(s32[8,1,192]{2,1,0:T(1,128)} %select_n.129), calls=%async_computation | async-start | bytes 16384 | tf_op jit(solution)/shard_map/all_to_all | solution.py:135
  196.6 39.5 %collective-permute-start.5 = (bf16[1,192,4096]{2,1,0:T(8,128)(2,1)}, bf16[1,192,4096]{2,1,0:T(8,128)(2,1)S(1)}, u32[]{:S(2)}, u32[]{:S(2)}) collective-permute-start(bf16[1,192,4096]{2,1,0:T(8,128)(2,1)} %get-tuple-element.1253), channel_id=1, source_target_pairs={{0,24},{4,28},{8,16},{12,20},{16,8},{20,12},{24,0},{28,4},{1,25},{... | collective-permute-start | bytes 4718600 | tf_op jit(solution)/shard_map/ppermute | solution.py:29
  203.0 64.0 %collective-permute-start.6 = (bf16[1,192,4096]{2,1,0:T(8,128)(2,1)}, bf16[1,192,4096]{2,1,0:T(8,128)(2,1)S(1)}, u32[]{:S(2)}, u32[]{:S(2)}) collective-permute-start(bf16[1,192,4096]{2,1,0:T(8,128)(2,1)} %get-tuple-element.1252), channel_id=1, source_target_pairs={{0,28},{4,24},{8,20},{12,16},{16,12},{20,8},{24,4},{28,0},{1,29},{... | collective-permute-start | bytes 4718600 | tf_op jit(solution)/shard_map/ppermute | solution.py:29
  268.2 11.0 copy-start.3
  279.2 718.5 %copy-start.2 = (f32[80,64]{1,0:T(8,128)S(1)}, f32[80,64]{1,0:T(8,128)}, u32[]{:S(2)}) copy-start(f32[80,64]{1,0:T(8,128)} %constant.2000.clone.1) | copy-start | bytes 61444
  279.2 718.5 %copy-start.4 = (f32[2,64]{1,0:T(2,128)S(1)}, f32[2,64]{1,0:T(2,128)}, u32[]{:S(2)}) copy-start(f32[2,64]{1,0:T(2,128)} %constant.2002.clone.1) | copy-start | bytes 1540
  279.2 718.5 %copy-start.5 = (f32[2,64]{1,0:T(2,128)S(1)}, f32[2,64]{1,0:T(2,128)}, u32[]{:S(2)}) copy-start(f32[2,64]{1,0:T(2,128)} %constant.2003.clone.1) | copy-start | bytes 1540
  1040.3 84.8 %all-to-all-start.1 = ((bf16[4,16,4096]{2,0,1:T(4,128)(2,1)}), bf16[4,16,4096]{2,0,1:T(4,128)(2,1)S(1)}, u32[]{:S(2)}, u32[]{:S(2)}) async-start(bf16[4,16,4096]{2,0,1:T(4,128)(2,1)} %copy.1305), calls=%async_computation.1 | async-start | bytes 1048576 | tf_op jit(solution)/shard_map/all_to_all | solution.py:167
